TPU v7x, 128 devices: a whole 4x4x4 slice. The times are simulated.
128 devices in a mesh: seg: 4 (over y_lo, core), item: 8 (over x, y_hi), slot: 4 (over z).
Axes of the slice: x: 4, y: 4 (y_hi: 2, y_lo: 2; y = y_hi * 2 + y_lo), z: 4, core: 2. Of those that a mesh axis runs over, the one named last changes fastest.
Arguments:
- tensor: float32 [128, 2048, 2048], P('slot', 'seg', 'item'), may hold values from -200 to 200
- b_factor: float32 [2048, 512], P('item'), may hold values from -25 to 25
- c_factor: float32 [128, 512], P('slot'), may hold values from -25 to 25
Outputs:
- a_factor: float32 [2048, 512], P('seg')
- b_new: float32 [2048, 512], P('item')
- lambda_a: float32 [512], replicated
- lambda_b: float32 [512], replicated
All inputs are finite; a program needn't handle non-finite values.
Results may differ from a plain program's by a relative error of at most 0.00027.
Values sent between devices are 32-bit elements; how exact they have to be, the bound alone decides.
No kernel may reach another device: no remote copies, remote signals or barrier semaphores. Data moves between devices by JAX's collectives and lax.ppermute only.
A program may use at most 128 MiB of HBM per device.

v0:
```python
import jax
import jax.numpy as jnp
from jax import lax
from jax.sharding import PartitionSpec as P

RIDGE_WEIGHT = 0.1
EPSILON = 1e-06
HIGHEST = lax.Precision.HIGHEST


def gram_of(row_block):
    return lax.dot_general(
        row_block,
        row_block,
        (((0,), (0,)), ((), ())),
        precision=HIGHEST,
        preferred_element_type=jnp.float32,
    )


def solve_rows(right_side, system):
    lower_factor = jnp.linalg.cholesky(system)
    half_solved = lax.linalg.triangular_solve(
        lower_factor, right_side, left_side=False, lower=True, transpose_a=True
    )
    return lax.linalg.triangular_solve(
        lower_factor, half_solved, left_side=False, lower=True, transpose_a=False
    )


def local(tensor, b_factor, c_factor):
    rank_width = b_factor.shape[1]
    seg_rows = tensor.shape[1]
    item_cols = tensor.shape[2]
    identity_matrix = jnp.eye(rank_width, dtype=jnp.float32)
    gram_b = lax.psum(gram_of(b_factor), "item")
    gram_c = lax.psum(gram_of(c_factor), "slot")
    system_one = gram_b * gram_c + RIDGE_WEIGHT * identity_matrix
    weighted_one = c_factor[:, None, :] * b_factor[None, :, :]
    row_total = lax.psum(
        jnp.einsum(
            "kij,kjr->ir",
            tensor,
            weighted_one,
            precision=HIGHEST,
            preferred_element_type=jnp.float32,
        ),
        ("item", "slot"),
    )
    segment_raw = solve_rows(row_total, system_one)
    rows_total = seg_rows * lax.axis_size("seg")
    squares = lax.psum(jnp.sum(segment_raw * segment_raw, axis=0), "seg")
    lambda_a = jnp.sqrt(squares / rows_total + EPSILON)
    a_factor = segment_raw / lambda_a[None, :]
    gram_a = lax.psum(gram_of(a_factor), "seg")
    system_two = gram_a * gram_c + RIDGE_WEIGHT * identity_matrix
    weighted_two = c_factor[:, None, :] * a_factor[None, :, :]
    col_partial = jnp.einsum(
        "kij,kir->jr", tensor, weighted_two, precision=HIGHEST, preferred_element_type=jnp.float32
    )
    col_total = lax.psum(col_partial, ("seg", "slot"))
    item_raw = solve_rows(col_total, system_two)
    item_squares = lax.psum(jnp.sum(item_raw * item_raw, axis=0), "item")
    lambda_b = jnp.sqrt(item_squares / (item_cols * lax.axis_size("item")) + EPSILON)
    b_new = item_raw / lambda_b[None, :]
    return (a_factor, b_new, lambda_a, lambda_b)


def solution(mesh):
    placed = (P("slot", "seg", "item"), P("item", None), P("slot", None))
    return jax.shard_map(
        local,
        mesh=mesh,
        in_specs=placed,
        out_specs=(P("seg", None), P("item", None), P(), P()),
        check_vma=False,
    )
```

profile of v0, /device:TPU:0, one launch (start us, length us, event | category | flops | bytes accessed | tf_op | source)
XLA Modules:
  0.0 754.6 jit_solution(1187668837796619864)
XLA Ops:
  7.2 3.0 fusion.113
  10.3 3.2 fusion.112
  13.6 1.2 copy.7
  14.8 31.3 %fusion.8 = f32[512,512]{0,1:T(8,128)} fusion(f32[32,512,256]{2,1,0:T(8,128)} %param.4, f32[256,512]{0,1:T(8,128)S(1)} %copy.7, f32[32,512]{1,0:T(8,128)} %param.6), kind=kOutput, calls=%fused_computation.14 | convolution fusion | flops 25773998080 | bytes 18415616 | tf_op jit(solution)/shard_map/kij,kjr->ir/dot_general | solution.py:41
  46.4 12.6 %all-reduce.11.cloned.1.call-done = f32[512,512]{0,1:T(8,128)} async-done(((f32[512,512]{0,1:T(8,128)}), f32[512,512]{0,1:T(8,128)}) %all-reduce.11.cloned.1.call-update) | async-done | bytes 1048592 | tf_op jit(solution)/shard_map/psum | solution.py:37
  59.0 91.9 %all-reduce.9.cloned.1.call-done = f32[512,512]{0,1:T(8,128)} async-done(((f32[512,512]{0,1:T(8,128)}), f32[512,512]{0,1:T(8,128)}) %all-reduce.9.cloned.1.call-update) | async-done | bytes 1048592 | tf_op jit(solution)/shard_map/psum | solution.py:36
  150.9 1.8 select_add_fusion.1
  153.2 11.7 %cholesky.286 = f32[128,128]{1,0:T(8,128)S(1)} custom-call(f32[128,128]{1,0:T(8,128)S(1)} %cholesky.426), custom_call_target="Cholesky" | custom-call | tf_op jit(solution)/shard_map/jit(cholesky)/cholesky | solution.py:22
  165.0 9.8 %custom-call.35 = f32[1,128,128]{1,2,0:T(8,128)S(1)} custom-call(f32[1,128,128]{2,1,0:T(8,128)S(1)} %get-tuple-element.64), custom_call_target="InvertDiagBlocksLowerTriangular" | custom-call | tf_op jit(solution)/shard_map/jit(cholesky)/cholesky | solution.py:22
  175.7 11.7 %cholesky.305 = f32[128,128]{1,0:T(8,128)S(1)} custom-call(f32[128,128]{1,0:T(8,128)S(1)} %cholesky.430), custom_call_target="Cholesky" | custom-call | tf_op jit(solution)/shard_map/jit(cholesky)/cholesky | solution.py:22
  187.6 10.0 %custom-call.36 = f32[1,128,128]{1,2,0:T(8,128)S(1)} custom-call(f32[1,128,128]{2,1,0:T(8,128)S(1)} %get-tuple-element.62), custom_call_target="InvertDiagBlocksLowerTriangular" | custom-call | tf_op jit(solution)/shard_map/jit(cholesky)/cholesky | solution.py:22
  198.7 11.7 %cholesky.326 = f32[128,128]{1,0:T(8,128)S(1)} custom-call(f32[128,128]{1,0:T(8,128)S(1)} %cholesky.435), custom_call_target="Cholesky" | custom-call | tf_op jit(solution)/shard_map/jit(cholesky)/cholesky | solution.py:22
  210.5 9.8 %custom-call.37 = f32[1,128,128]{1,2,0:T(8,128)S(1)} custom-call(f32[1,128,128]{2,1,0:T(8,128)S(1)} %get-tuple-element.60), custom_call_target="InvertDiagBlocksLowerTriangular" | custom-call | tf_op jit(solution)/shard_map/jit(cholesky)/cholesky | solution.py:22
  221.1 12.1 %cholesky.343 = f32[128,128]{1,0:T(8,128)S(1)} custom-call(f32[128,128]{1,0:T(8,128)S(1)} %convolution_subtract_fusion.17), custom_call_target="Cholesky" | custom-call | tf_op jit(solution)/shard_map/jit(cholesky)/cholesky | solution.py:22
  238.1 8.9 %while.2 = (s32[]{:T(128)}, f32[512,512]{0,1:T(8,128)S(1)}, s32[4,2]{0,1:T(2,128)S(1)}, f32[4,128,128]{2,1,0:T(8,128)S(1)}, s32[]{:T(128)}) while((s32[]{:T(128)}, f32[512,512]{0,1:T(8,128)S(1)}, s32[4,2]{0,1:T(2,128)S(1)}, f32[4,128,128]{2,1,0:T(8,128)S(1)}, s32[]{:T(128)}) %tuple.48), condition=%wide.while_cond, body=%wide.while_body.sunk | while | flops 2 | bytes 393321 | solution.py:23
  238.8 1.4 dynamic-slice.13
  241.0 1.4 dynamic-slice.13
  243.2 1.4 dynamic-slice.13
  245.5 1.4 dynamic-slice.13
  247.0 39.3 %custom-call.30 = f32[4,128,128]{1,2,0:T(8,128)S(1)} custom-call(f32[4,128,128]{2,1,0:T(8,128)S(1)} %get-tuple-element.12), custom_call_target="InvertDiagBlocksLowerTriangular" | custom-call | tf_op jit(solution)/shard_map/triangular_solve | solution.py:23
  286.4 219.1 %all-reduce.7.cloned.1.call-done = f32[512,512]{0,1:T(8,128)} async-done(((f32[512,512]{0,1:T(8,128)}), f32[512,512]{0,1:T(8,128)}) %all-reduce.7.cloned.1.call-update) | async-done | bytes 1048592 | tf_op jit(solution)/shard_map/psum | solution.py:40
  505.5 1.4 fusion.46
  506.9 1.4 convolution_subtract_fusion.3
  508.6 1.4 convolution_subtract_fusion.2
  510.5 1.6 convolution_subtract_fusion.5
  516.0 6.0 psum.52
  522.1 2.8 fusion.114
  525.0 11.0 %fusion.146 = f32[32,512,512]{1,2,0:T(8,128)} fusion(f32[512,512]{0,1:T(8,128)S(1)} %fusion.26, f32[32,512]{1,0:T(8,128)S(1)} %copy-done.1), kind=kLoop, calls=%fused_computation.5.clone.clone.clone.1 | loop fusion | flops 8388608 | bytes 34668544 | tf_op jit(solution)/shard_map/kij,kir->jr/dot_general | solution.py:58
  536.0 1.3 copy.29
  537.6 32.5 %fusion.11 = f32[256,512]{0,1:T(8,128)} fusion(f32[32,512,256]{2,1,0:T(8,128)} %param.4, f32[32,512,512]{1,2,0:T(8,128)} %fusion.146), kind=kOutput, calls=%fused_computation.15 | convolution fusion | flops 25769803776 | bytes 50855936 | tf_op jit(solution)/shard_map/kij,kir->jr/dot_general | solution.py:58
  570.1 8.7 %all-reduce.15.cloned.1.call-done = f32[512,512]{0,1:T(8,128)} async-done(((f32[512,512]{0,1:T(8,128)}), f32[512,512]{0,1:T(8,128)}) %all-reduce.15.cloned.1.call-update) | async-done | bytes 1048592 | tf_op jit(solution)/shard_map/psum | solution.py:55
  578.9 1.4 select_add_fusion
  580.9 11.7 %cholesky.358 = f32[128,128]{1,0:T(8,128)S(1)} custom-call(f32[128,128]{1,0:T(8,128)S(1)} %cholesky.439), custom_call_target="Cholesky" | custom-call | tf_op jit(solution)/shard_map/jit(cholesky)/cholesky | solution.py:22
  592.7 9.8 %custom-call.38 = f32[1,128,128]{1,2,0:T(8,128)S(1)} custom-call(f32[1,128,128]{2,1,0:T(8,128)S(1)} %get-tuple-element.58), custom_call_target="InvertDiagBlocksLowerTriangular" | custom-call | tf_op jit(solution)/shard_map/jit(cholesky)/cholesky | solution.py:22
  603.1 11.7 %cholesky.377 = f32[128,128]{1,0:T(8,128)S(1)} custom-call(f32[128,128]{1,0:T(8,128)S(1)} %cholesky.443), custom_call_target="Cholesky" | custom-call | tf_op jit(solution)/shard_map/jit(cholesky)/cholesky | solution.py:22
  615.2 10.2 %custom-call.39 = f32[1,128,128]{1,2,0:T(8,128)S(1)} custom-call(f32[1,128,128]{2,1,0:T(8,128)S(1)} %get-tuple-element.56), custom_call_target="InvertDiagBlocksLowerTriangular" | custom-call | tf_op jit(solution)/shard_map/jit(cholesky)/cholesky | solution.py:22
  626.5 11.7 %cholesky.398 = f32[128,128]{1,0:T(8,128)S(1)} custom-call(f32[128,128]{1,0:T(8,128)S(1)} %cholesky.448), custom_call_target="Cholesky" | custom-call | tf_op jit(solution)/shard_map/jit(cholesky)/cholesky | solution.py:22
  638.4 9.8 %custom-call.40 = f32[1,128,128]{1,2,0:T(8,128)S(1)} custom-call(f32[1,128,128]{2,1,0:T(8,128)S(1)} %get-tuple-element.54), custom_call_target="InvertDiagBlocksLowerTriangular" | custom-call | tf_op jit(solution)/shard_map/jit(cholesky)/cholesky | solution.py:22
  649.0 11.9 %cholesky.415 = f32[128,128]{1,0:T(8,128)S(1)} custom-call(f32[128,128]{1,0:T(8,128)S(1)} %convolution_subtract_fusion.16), custom_call_target="Cholesky" | custom-call | tf_op jit(solution)/shard_map/jit(cholesky)/cholesky | solution.py:22
  666.4 8.6 %while.3 = (s32[]{:T(128)}, f32[512,512]{0,1:T(8,128)S(1)}, s32[4,2]{0,1:T(2,128)S(1)}, f32[4,128,128]{2,1,0:T(8,128)S(1)}, s32[]{:T(128)}) while((s32[]{:T(128)}, f32[512,512]{0,1:T(8,128)S(1)}, s32[4,2]{0,1:T(2,128)S(1)}, f32[4,128,128]{2,1,0:T(8,128)S(1)}, s32[]{:T(128)}) %tuple.64), condition=%wide.while_cond.1, body=%wide.while_body.1.sunk | while | flops 2 | bytes 393321 | solution.py:23
  667.1 1.3 dynamic-slice.15
  669.2 1.3 dynamic-slice.15
  671.4 1.3 dynamic-slice.15
  673.5 1.3 dynamic-slice.15
  675.0 39.3 %custom-call.31 = f32[4,128,128]{1,2,0:T(8,128)S(1)} custom-call(f32[4,128,128]{2,1,0:T(8,128)S(1)} %get-tuple-element.20), custom_call_target="InvertDiagBlocksLowerTriangular" | custom-call | tf_op jit(solution)/shard_map/triangular_solve | solution.py:23
  717.2 1.3 convolution_subtract_fusion.11
  718.8 1.4 convolution_subtract_fusion.10
  722.9 23.8 %psum.55 = f32[512]{0:T(512)S(1)} all-reduce(f32[512]{0:T(512)S(1)} %multiply_reduce_fusion.1), channel_id=1, replica_groups=mesh['seg'=4,'item'=8,'slot'=4] {'item'}, use_global_device_ids=true, to_apply=%region_16.18 | all-reduce | flops 512 | bytes 4096 | tf_op jit(solution)/shard_map/psum | solution.py:63
  (143 shorter events, 30.9 us)
Async XLA Ops:
  7.2 51.8 %all-reduce.11.cloned.1.call-start = ((), (), s32[]{:S(2)}) async-start(), calls=%async_computation.2 | async-start | bytes 2097152 | tf_op jit(solution)/shard_map/psum | solution.py:37
  10.2 140.7 %all-reduce.9.cloned.1.call-start = ((), (), s32[]{:S(2)}) async-start(), calls=%async_computation.1 | async-start | bytes 2097152 | tf_op jit(solution)/shard_map/psum | solution.py:36
  13.5 492.0 %all-reduce.7.cloned.1.call-start = ((), (), s32[]{:S(2)}) async-start(), calls=%async_computation | async-start | bytes 2097152 | tf_op jit(solution)/shard_map/psum | solution.py:40
  46.2 532.7 %all-reduce.15.cloned.1.call-start = ((), (), s32[]{:S(2)}) async-start(), calls=%async_computation.4 | async-start | bytes 2097152 | tf_op jit(solution)/shard_map/psum | solution.py:55
  152.6 372.3 %copy-start.1 = (f32[32,512]{1,0:T(8,128)S(1)}, f32[32,512]{1,0:T(8,128)}, u32[]{:S(2)}) copy-start(f32[32,512]{1,0:T(8,128)} %param.6) | copy-start | bytes 196612
  522.0 14.0 %copy-start.2 = (f32[512]{0:T(512)}, f32[512]{0:T(512)S(1)}, u32[]{:S(2)}) copy-start(f32[512]{0:T(512)S(1)} %add_sqrt_fusion.1) | copy-start | bytes 6148
  537.4 41.5 %copy-start = (f32[512,512]{0,1:T(8,128)S(1)}, f32[512,512]{0,1:T(8,128)}, u32[]{:S(2)}) copy-start(f32[512,512]{0,1:T(8,128)} %all-reduce.11.cloned.1.call-done) | copy-start | bytes 3145732
  537.4 177.0 %all-reduce.13.cloned.1.call-start = ((), (), s32[]{:S(2)}) async-start(), calls=%async_computation.3 | async-start | bytes 1048576 | tf_op jit(solution)/shard_map/psum | solution.py:61
  746.7 1.2 copy-start.3
Sparse Core Ops, SparseCore 0:
  10.4 48.5 all-reduce.10
  61.6 89.2 all-reduce.8
  154.1 351.3 all-reduce.6
  537.5 41.3 all-reduce.14
  581.9 120.8 all-reduce.12
where the time goes:
time: 760 us; the launch traced here: 755 us
  waiting for transfers between devices  332 us (44%)
  other arithmetic  253 us (33%)
  matrix products  96 us (13%)
  blocking collectives  29.8 us (4%)
  local copies, waits for them, and re-layouts  22.9 us (3%)
  between operations  19.7 us (3%)
    psum x1, waiting for transfers between devices, local(): lax.psum(jnp.einsum('kij,kjr->ir', tensor, weighted_one, precision=HIGHES...  219 us
    another operation x29, other arithmetic, solve_rows(): lower_factor = jnp.linalg.cholesky(system)  159 us
    psum x1, waiting for transfers between devices, local(): gram_b = lax.psum(gram_of(b_factor), 'item')  91.9 us
    another operation x5, other arithmetic, solve_rows(): lax.linalg.triangular_solve(lower_factor, right_side, left_side=False, lo...  78.9 us
    dot_general x1, matrix products, local(): jnp.einsum('kij,kir->jr', tensor, weighted_two, precision=HIGHEST, prefer...  32.5 us
    dot_general x1, matrix products, local(): jnp.einsum('kij,kjr->ir', tensor, weighted_one, precision=HIGHEST, prefer...  31.3 us
    psum x1, blocking collectives, local(): item_squares = lax.psum(jnp.sum(item_raw * item_raw, axis=0), 'item')  23.8 us
    another operation x40, local copies, waits for them, and re-layouts  17.3 us
  transfers between devices with their start and end apart: 5, of which 4 were waited for; matrix products, arithmetic and copies ran while one was open for 44% of the time, Pallas kernels for 0%

commit v1 on v0

v1 whole, which is shorter than its diff:
```python
import functools

import jax
import jax.numpy as jnp
from jax import lax
from jax.experimental import pallas as pl
from jax.experimental.pallas import tpu as pltpu
from jax.sharding import PartitionSpec as P

RIDGE_WEIGHT = 0.1
EPSILON = 1e-06
HIGHEST = lax.Precision.HIGHEST
BLOCK = 128
PANEL = 16
STEP = 8
VMEM = pl.BlockSpec(memory_space=pltpu.VMEM)
PARAMS = pltpu.CompilerParams(vmem_limit_bytes=48 * 1024 * 1024)


def dot_full(left, right, left_dim=1):
    return lax.dot_general(
        left, right, (((left_dim,), (0,)), ((), ())), precision=HIGHEST, preferred_element_type=jnp.float32
    )


def split_two(values):
    high = values.astype(jnp.bfloat16)
    return high, (values - high.astype(jnp.float32)).astype(jnp.bfloat16)


def strip_place(strip):
    return ((0, 0), (1, 0), (1, 3 * BLOCK), (0, 4 * BLOCK))[strip]


def store_gram(rows, strips_ref):
    width = rows.shape[1]
    for strip in range(width // BLOCK):
        slab, start = strip_place(strip)
        low = strip * BLOCK
        strips_ref[slab, :, start:start + width - low] = dot_full(rows[:, low:low + BLOCK], rows[:, low:], 0)


def gram_kernel(rows_ref, strips_ref):
    store_gram(rows_ref[...], strips_ref)


def strips_shape(width):
    return jax.ShapeDtypeStruct((2, BLOCK, width + BLOCK), jnp.float32)


def gram_strips(rows):
    return pl.pallas_call(
        gram_kernel,
        out_shape=strips_shape(rows.shape[1]),
        in_specs=[VMEM],
        out_specs=VMEM,
        compiler_params=PARAMS,
    )(rows)


def contraction_kernel(slab_ref, factor_ref, weight_ref, start_ref, out_ref, parts_ref, *, contract, fresh):
    depth = factor_ref.shape[0]

    @pl.when(pl.program_id(0) == 0)
    def _():
        high, low = split_two(factor_ref[...])
        parts_ref[0:depth, :] = high
        parts_ref[depth:2 * depth, :] = high
        parts_ref[2 * depth:3 * depth, :] = low
        out_ref[...] = jnp.zeros_like(out_ref) if fresh else start_ref[...]

    for k in range(STEP):
        high, low = split_two(slab_ref[k])
        pieces = jnp.concatenate([high, low, high], axis=contract)
        term = lax.dot_general(
            pieces, parts_ref[...], (((contract,), (0,)), ((), ())), preferred_element_type=jnp.float32
        )
        out_ref[...] += term * weight_ref[0, k:k + 1, :]


def contraction(tensor, factor, weights, contract, first, last, start=None):
    slots, rows, cols = tensor.shape
    depth, width = factor.shape
    out_rows = rows if contract == 1 else cols
    fresh = start is None
    if fresh:
        start = jnp.zeros((8, 128), jnp.float32)
    count = last - first
    weights = weights.reshape(slots // STEP, STEP, width)
    return pl.pallas_call(
        functools.partial(contraction_kernel, contract=contract, fresh=fresh),
        grid=(count,),
        in_specs=[
            pl.BlockSpec((STEP, rows, cols), lambda g: (g + first, 0, 0)),
            pl.BlockSpec((depth, width), lambda g: (0, 0)),
            pl.BlockSpec((1, STEP, width), lambda g: (g + first, 0, 0)),
            pl.BlockSpec(start.shape, lambda g: (0, 0)),
        ],
        out_specs=pl.BlockSpec((out_rows, width), lambda g: (0, 0)),
        out_shape=jax.ShapeDtypeStruct((out_rows, width), jnp.float32),
        scratch_shapes=[pltpu.VMEM((3 * depth, width), jnp.bfloat16)],
        compiler_params=PARAMS,
        cost_estimate=pl.CostEstimate(
            flops=9 * count * STEP * rows * cols * width,
            bytes_accessed=count * STEP * rows * cols * 4,
            transcendentals=0,
        ),
    )(tensor, factor, weights, start)


def invert_block(block):
    size = block.shape[0]
    shape = (PANEL, size)
    sub = lax.broadcasted_iota(jnp.int32, shape, 0)
    lane = lax.broadcasted_iota(jnp.int32, shape, 1)
    row_index = lax.broadcasted_iota(jnp.int32, (size, size), 0)
    col_index = lax.broadcasted_iota(jnp.int32, (size, size), 1)
    for low in range(0, size, PANEL):
        high = low + PANEL
        panel = block[low:high, :]
        columns = [jnp.broadcast_to(panel[:, low + t:low + t + 1], shape) for t in range(PANEL)]
        result = jnp.where((lane >= low) & (lane < high), jnp.where(lane - low == sub, 1.0, 0.0), panel)
        for t in range(PANEL):
            here = sub == t
            column = columns[t]
            scale = 1.0 / column[t:t + 1, :]
            for u in range(t + 1, PANEL):
                pivot = columns[u][t:t + 1, :] * scale
                columns[u] = jnp.where(here, jnp.broadcast_to(pivot, shape), columns[u] - column * pivot)
            pivot = result[t:t + 1, :] * scale
            result = jnp.where(here, jnp.broadcast_to(pivot, shape), result - column * pivot)
        parts = [result]
        if low:
            parts.insert(0, jnp.zeros((low, size), jnp.float32))
        if high < size:
            parts.append(jnp.zeros((size - high, size), jnp.float32))
        padded = jnp.concatenate(parts, axis=0)
        update = dot_full(block, padded)
        kept = jnp.where((col_index >= low) & (col_index < high), 0.0, block)
        block = jnp.where((row_index >= low) & (row_index < high), padded, kept - update)
    return block


def eliminate(matrix_ref, first, last):
    size = matrix_ref.shape[0]

    def step(p, carry):
        low = pl.multiple_of(p * BLOCK, BLOCK)
        here = pl.ds(low, BLOCK)
        inverse = invert_block(matrix_ref[here, here])
        column = matrix_ref[:, here]
        matrix_ref[:, here] = jnp.zeros((size, BLOCK), jnp.float32)
        matrix_ref[here, here] = jnp.eye(BLOCK, dtype=jnp.float32)
        row = dot_full(inverse, matrix_ref[here, :])
        matrix_ref[...] = matrix_ref[...] - dot_full(column, row)
        matrix_ref[here, :] = row
        return carry

    lax.fori_loop(first, last, step, 0)


def first_half_kernel(strips_ref, slots_ref, matrix_ref, scale_ref, *, rows_total):
    size = matrix_ref.shape[0]
    blocks = size // BLOCK
    diagonal = lax.broadcasted_iota(jnp.int32, (BLOCK, BLOCK), 0) == lax.broadcasted_iota(
        jnp.int32, (BLOCK, BLOCK), 1
    )
    if rows_total is None:
        scale_ref[...] = jnp.ones_like(scale_ref)
    else:
        for p in range(blocks):
            slab, start = strip_place(p)
            squares = jnp.where(diagonal, strips_ref[slab, :, start:start + BLOCK], 0.0)
            scale_ref[:, p * BLOCK:(p + 1) * BLOCK] = jnp.sqrt(
                jnp.sum(squares, axis=0, keepdims=True) / rows_total + EPSILON
            )
    for p in range(blocks):
        slab, start = strip_place(p)
        low = p * BLOCK
        gram = strips_ref[slab, :, start:start + size - low]
        if rows_total is not None:
            squares = jnp.where(diagonal, gram[:, 0:BLOCK], 0.0)
            scale = jnp.sqrt(jnp.sum(squares, axis=1, keepdims=True) / rows_total + EPSILON)
            gram = gram / scale / scale_ref[:, low:]
        system = gram * dot_full(slots_ref[:, low:low + BLOCK], slots_ref[:, low:], 0)
        matrix_ref[low:low + BLOCK, low:] = system
        matrix_ref[low:low + BLOCK, low:low + BLOCK] = system[:, 0:BLOCK] + jnp.where(diagonal, RIDGE_WEIGHT, 0.0)
        for q in range(p + 1, blocks):
            matrix_ref[q * BLOCK:(q + 1) * BLOCK, low:low + BLOCK] = system[
                :, (q - p) * BLOCK:(q - p + 1) * BLOCK
            ].T
    eliminate(matrix_ref, 0, blocks // 2)


def first_half(strips, slots_all, rows_total):
    size = slots_all.shape[1]
    return pl.pallas_call(
        functools.partial(first_half_kernel, rows_total=rows_total),
        out_shape=(
            jax.ShapeDtypeStruct((size, size), jnp.float32),
            jax.ShapeDtypeStruct((1, size), jnp.float32),
        ),
        in_specs=[VMEM, VMEM],
        out_specs=(VMEM, VMEM),
        compiler_params=PARAMS,
        cost_estimate=pl.CostEstimate(flops=12 * 10**9, bytes_accessed=2**20, transcendentals=0),
    )(strips, slots_all)


def second_half_kernel(matrix_ref, out_ref):
    blocks = matrix_ref.shape[0] // BLOCK
    out_ref[...] = matrix_ref[...]
    eliminate(out_ref, blocks // 2, blocks)


def second_half(matrix):
    return pl.pallas_call(
        second_half_kernel,
        out_shape=jax.ShapeDtypeStruct(matrix.shape, jnp.float32),
        in_specs=[VMEM],
        out_specs=VMEM,
        compiler_params=PARAMS,
        cost_estimate=pl.CostEstimate(flops=12 * 10**9, bytes_accessed=2**20, transcendentals=0),
    )(matrix)


def solve_one_kernel(total_ref, inverse_ref, raw_ref, strips_ref):
    raw = dot_full(total_ref[...], inverse_ref[...])
    raw_ref[...] = raw
    store_gram(raw, strips_ref)


def solve_one(total, inverse):
    return pl.pallas_call(
        solve_one_kernel,
        out_shape=(jax.ShapeDtypeStruct(total.shape, jnp.float32), strips_shape(total.shape[1])),
        in_specs=[VMEM, VMEM],
        out_specs=(VMEM, VMEM),
        compiler_params=PARAMS,
    )(total, inverse)


def solve_two_kernel(total_ref, scale_ref, inverse_ref, raw_ref, squares_ref):
    raw = dot_full(total_ref[...] / scale_ref[...], inverse_ref[...])
    raw_ref[...] = raw
    squares_ref[...] = jnp.sum(raw * raw, axis=0, keepdims=True)


def solve_two(total, scale, inverse):
    return pl.pallas_call(
        solve_two_kernel,
        out_shape=(
            jax.ShapeDtypeStruct(total.shape, jnp.float32),
            jax.ShapeDtypeStruct((1, total.shape[1]), jnp.float32),
        ),
        in_specs=[VMEM, VMEM, VMEM],
        out_specs=(VMEM, VMEM),
        compiler_params=PARAMS,
    )(total, scale, inverse)


def exchange(values, axes):
    return lax.all_to_all(values, axes, 0, 0, tiled=True)


def scattered_sum(received, parts):
    rows, cols = received.shape
    return jnp.sum(received.reshape(parts, rows // parts, cols), axis=0)


def spread(values, axes, parts):
    rows, cols = values.shape
    copies = jnp.broadcast_to(values[None], (parts, rows, cols)).reshape(parts * rows, cols)
    return exchange(copies, axes)


def swap(values, axis, mask):
    return lax.ppermute(values, axis, [(i, i ^ mask) for i in range(lax.axis_size(axis))])


def local(tensor, b_factor, c_factor):
    width = b_factor.shape[1]
    segs, items, slots = (lax.axis_size(name) for name in ("seg", "item", "slot"))
    steps = tensor.shape[0] // STEP
    slab_rows = width + BLOCK

    slots_all = spread(c_factor, "slot", slots)
    b_strips = gram_strips(b_factor).reshape(2 * BLOCK, slab_rows)
    b_received = exchange(b_strips, "item")
    one = contraction(tensor, b_factor, c_factor, 1, 0, steps)
    b_received, one = lax.optimization_barrier((b_received, one))
    b_strips = spread(scattered_sum(b_received, items), "item", items).reshape(2, BLOCK, slab_rows)
    one_received = exchange(one, ("item", "slot"))

    matrix, unused = first_half(b_strips, slots_all, None)
    matrix, one_received = lax.optimization_barrier((matrix, one_received))
    one_total = spread(scattered_sum(one_received, items * slots), ("item", "slot"), items * slots)
    inverse = second_half(matrix)
    segment_raw, a_strips = solve_one(one_total, inverse)

    core = lax.axis_index("seg") % 2
    mine = lax.dynamic_index_in_dim(a_strips, core, 0, keepdims=False)
    other = lax.dynamic_index_in_dim(a_strips, 1 - core, 0, keepdims=False)
    arrived = swap(other, "seg", 1)
    two = contraction(tensor, segment_raw, c_factor, 0, 0, 1)
    arrived, two = lax.optimization_barrier((arrived, two))
    mine = mine + arrived
    arrived = swap(mine, "seg", 2)
    two = contraction(tensor, segment_raw, c_factor, 0, 1, 3, two)
    arrived, two = lax.optimization_barrier((arrived, two))
    mine = mine + arrived
    arrived = swap(mine, "seg", 1)
    two = contraction(tensor, segment_raw, c_factor, 0, 3, steps, two)
    a_strips = jnp.where(core == 0, jnp.stack([mine, arrived]), jnp.stack([arrived, mine]))

    two_received = exchange(two, ("seg", "slot"))
    matrix, scale = first_half(a_strips, slots_all, tensor.shape[1] * segs)
    matrix, two_received = lax.optimization_barrier((matrix, two_received))
    two_total = spread(scattered_sum(two_received, segs * slots), ("seg", "slot"), segs * slots)
    inverse = second_half(matrix)
    a_factor = segment_raw / scale
    item_raw, squares = solve_two(two_total, scale, inverse)
    squares = jnp.sum(spread(squares, "item", items), axis=0)
    lambda_b = jnp.sqrt(squares / (tensor.shape[2] * items) + EPSILON)
    b_new = item_raw / lambda_b[None, :]
    return (a_factor, b_new, scale.reshape(width), lambda_b)


def solution(mesh):
    placed = (P("slot", "seg", "item"), P("item", None), P("slot", None))
    return jax.shard_map(
        local,
        mesh=mesh,
        in_specs=placed,
        out_specs=(P("seg", None), P("item", None), P(), P()),
        check_vma=False,
    )
```

time: 760 us -> 182 us (0.24)
  waiting for transfers between devices: 332 us -> 23.4 us
  other arithmetic: 253 us -> 2.29 us
  matrix products: 96 us -> 0 us
  Pallas kernels: 0 us -> 85.3 us
  starting transfers between devices: 0.55 us -> 38.1 us
  between operations: 19.7 us -> 0.93 us
  local copies, waits for them, and re-layouts: 22.9 us -> 11.6 us
  blocking collectives: 29.8 us -> 19.6 us
    psum x5 -> x0, waiting for transfers between devices: 332 us -> none  [the longest x1 219 us: local(): lax.psum(jnp.einsum('kij,kjr->ir', tensor, weighted_one, precision=HIGHES...]
    another operation x34 -> x0, other arithmetic: 238 us -> none  [the longest x29 159 us: solve_rows(): lower_factor = jnp.linalg.cholesky(system)]
    pallas_call x0 -> x11, Pallas kernels: none -> 85.3 us  [the longest x4 38.7 us: contraction(): pl.pallas_call(functools.partial(contraction_kernel, contract=contract, f...]
    dot_general x5 -> x0, matrix products: 72.9 us -> none  [the longest x1 32.5 us: local(): jnp.einsum('kij,kir->jr', tensor, weighted_two, precision=HIGHEST, prefer...]
    all_to_all x0 -> x7, starting transfers between devices: none -> 35.3 us  [exchange(): return lax.all_to_all(values, axes, 0, 0, tiled=True)]
    psum x2 -> x0, blocking collectives: 29.8 us -> none  [the longest x1 23.8 us: local(): item_squares = lax.psum(jnp.sum(item_raw * item_raw, axis=0), 'item')]
    all_to_all x0 -> x7, waiting for transfers between devices: none -> 23.4 us  [exchange(): return lax.all_to_all(values, axes, 0, 0, tiled=True)]
    another operation x40 -> x0, matrix products: 23.1 us -> none  [the longest x14 13.3 us: solve_rows(): lax.linalg.triangular_solve(lower_factor, right_side, left_side=False, lo...]
  transfers between devices with their start and end apart: 5 -> 10, of which waited for: 4 -> 4; matrix products, arithmetic and copies ran while one was open for 44% -> 1% of each run, Pallas kernels for 0% -> 44%
where the time goes in v1:
time: 182 us; the launch traced here: 181 us
  Pallas kernels  85.3 us (47%)
  starting transfers between devices  38.1 us (21%)
  waiting for transfers between devices  23.4 us (13%)
  blocking collectives  19.6 us (11%)
  local copies, waits for them, and re-layouts  11.6 us (6%)
  other arithmetic  2.29 us (1%)
    pallas_call x4, Pallas kernels, contraction(): pl.pallas_call(functools.partial(contraction_kernel, contract=contract, f...  38.7 us
    all_to_all x7, starting transfers between devices, exchange(): return lax.all_to_all(values, axes, 0, 0, tiled=True)  35.3 us
    all_to_all x7, waiting for transfers between devices, exchange(): return lax.all_to_all(values, axes, 0, 0, tiled=True)  23.4 us
    pallas_call x2, Pallas kernels, first_half(): pl.pallas_call(functools.partial(first_half_kernel, rows_total=rows_total...  21.5 us
    pallas_call x2, Pallas kernels, second_half(): pl.pallas_call(second_half_kernel, out_shape=jax.ShapeDtypeStruct(matrix....  19.9 us
    all_to_all x1, blocking collectives, exchange(): return lax.all_to_all(values, axes, 0, 0, tiled=True)  19.6 us
    unnamed x20, local copies, waits for them, and re-layouts  6.43 us
    broadcast_in_dim x4, local copies, waits for them, and re-layouts, spread(): jnp.broadcast_to(values[None], (parts, rows, cols))  4.55 us
  transfers between devices with their start and end apart: 10, of which 4 were waited for; matrix products, arithmetic and copies ran while one was open for 1% of the time, Pallas kernels for 44%

profile of v1, /device:TPU:0, one launch (start us, length us, event | category | flops | bytes accessed | tf_op | source)
XLA Modules:
  0.0 181.2 jit_solution(9190282807762999831)
XLA Ops:
  0.6 0.0 copy-start.2
  0.6 1.0 copy-done.2
  1.7 0.9 shard_map.66
  2.6 19.6 %all_to_all.72 = f32[8,32,640]{2,1,0:T(8,128)S(1)} all-to-all(f32[8,32,640]{2,1,0:T(8,128)S(1)} %bitcast.23), channel_id=1, replica_groups=mesh['seg'=4,'item'=8,'slot'=4] {'item'}, dimensions={0} | all-to-all | bytes 1310720 | tf_op jit(solution)/shard_map/all_to_all | solution.py:263
  22.2 1.6 broadcast_in_dim.9
  23.8 5.3 %all-to-all-start.2 = ((f32[4,32,512]{2,1,0:T(8,128)}), f32[4,32,512]{2,1,0:T(8,128)S(1)}, u32[]{:S(2)}, u32[]{:S(2)}) async-start(f32[4,32,512]{2,1,0:T(8,128)} %broadcast_in_dim.9), calls=%async_computation.2 | async-start | bytes 524288 | tf_op jit(solution)/shard_map/all_to_all | solution.py:263
  29.1 0.8 copy-done
  29.9 1.0 copy-done.3
  30.9 17.2 %shard_map.67 = f32[512,512]{1,0:T(8,128)} custom-call(f32[32,512,256]{2,1,0:T(8,128)} %slab_ref.7, f32[256,512]{1,0:T(8,128)S(1)} %copy-done.3, f32[4,8,512]{2,1,0:T(8,128)S(1)} %bitcast.26, f32[8,128]{1,0:T(8,128)S(1)} %broadcast_1_start_ref.2.start_ref), custom_call_target="tpu_custom_call" | custom-call | flops 19327352832 | bytes 16777216 | tf_op jit(solution)/shard_map/pallas_call | solution.py:90
  48.2 0.0 all-to-all-done.2
  48.2 0.9 broadcast_in_dim.8
  49.1 3.5 %all-to-all-start.1 = ((f32[8,32,640]{2,1,0:T(8,128)}), f32[8,32,640]{2,1,0:T(8,128)S(1)}, u32[]{:S(2)}, u32[]{:S(2)}) async-start(f32[8,32,640]{2,1,0:T(8,128)} %broadcast_in_dim.8), calls=%async_computation.1 | async-start | bytes 1310720 | tf_op jit(solution)/shard_map/all_to_all | solution.py:263
  52.6 10.6 %all-to-all-done.1 = f32[8,32,640]{2,1,0:T(8,128)S(1)} async-done(((f32[8,32,640]{2,1,0:T(8,128)}), f32[8,32,640]{2,1,0:T(8,128)S(1)}, u32[]{:S(2)}, u32[]{:S(2)}) %all-to-all-start.1) | async-done | bytes 655392 | tf_op jit(solution)/shard_map/all_to_all | solution.py:263
  63.3 6.3 %all-to-all-start.3 = ((f32[32,16,512]{2,1,0:T(8,128)}), f32[32,16,512]{2,1,0:T(8,128)S(1)}, u32[]{:S(2)}, u32[]{:S(2)}) async-start(f32[32,16,512]{2,1,0:T(8,128)} %bitcast.6), calls=%async_computation.3 | async-start | bytes 2097152 | tf_op jit(solution)/shard_map/all_to_all | solution.py:263
  69.6 10.7 %shard_map.68 = (f32[512,512]{1,0:T(8,128)S(1)}, f32[1,512]{1,0:T(1,128)}) custom-call(f32[2,128,640]{2,1,0:T(8,128)S(1)} %bitcast.25, f32[128,512]{1,0:T(8,128)S(1)} %bitcast.30), custom_call_target="tpu_custom_call" | custom-call | flops 12000000000 | bytes 1048576 | tf_op jit(solution)/shard_map/pallas_call | solution.py:197
  80.4 1.0 copy-done.7
  81.3 3.2 %all-to-all-done.3 = f32[32,16,512]{2,1,0:T(8,128)S(1)} async-done(((f32[32,16,512]{2,1,0:T(8,128)}), f32[32,16,512]{2,1,0:T(8,128)S(1)}, u32[]{:S(2)}, u32[]{:S(2)}) %all-to-all-start.3) | async-done | bytes 1048608 | tf_op jit(solution)/shard_map/all_to_all | solution.py:263
  84.5 0.1 reduce_sum.37
  84.6 1.1 broadcast_in_dim.10
  85.7 6.8 %all-to-all-start.4 = ((f32[32,16,512]{2,1,0:T(8,128)}), f32[32,16,512]{2,1,0:T(8,128)S(1)}, u32[]{:S(2)}, u32[]{:S(2)}) async-start(f32[32,16,512]{2,1,0:T(8,128)} %broadcast_in_dim.10), calls=%async_computation.4 | async-start | bytes 2097152 | tf_op jit(solution)/shard_map/all_to_all | solution.py:263
  92.5 1.2 copy-done.8
  93.7 10.0 %shard_map.69.inverse_ref = f32[512,512]{1,0:T(8,128)S(1)} custom-call(f32[512,512]{1,0:T(8,128)S(1)} %copy-done.8), custom_call_target="tpu_custom_call" | custom-call | flops 12000000000 | bytes 1048576 | tf_op jit(solution)/shard_map/pallas_call | solution.py:217
  103.7 3.0 %all-to-all-done.4 = f32[32,16,512]{2,1,0:T(8,128)S(1)} async-done(((f32[32,16,512]{2,1,0:T(8,128)}), f32[32,16,512]{2,1,0:T(8,128)S(1)}, u32[]{:S(2)}, u32[]{:S(2)}) %all-to-all-start.4) | async-done | bytes 1048608 | tf_op jit(solution)/shard_map/all_to_all | solution.py:263
  106.6 3.3 %shard_map.70 = (f32[512,512]{1,0:T(8,128)S(1)}, f32[2,128,640]{2,1,0:T(8,128)S(1)}) custom-call(f32[512,512]{1,0:T(8,128)S(1)} %bitcast.22, f32[512,512]{1,0:T(8,128)S(1)} %shard_map.69.inverse_ref), custom_call_target="tpu_custom_call" | custom-call | tf_op jit(solution)/shard_map/pallas_call | solution.py:234
  110.0 0.1 collective-permute-start
  110.1 5.7 %shard_map.71.start_ref = f32[256,512]{1,0:T(8,128)S(1)} custom-call(f32[32,512,256]{2,1,0:T(8,128)} %slab_ref.7, f32[512,512]{1,0:T(8,128)S(1)} %get-tuple-element.26.factor_ref, f32[4,8,512]{2,1,0:T(8,128)S(1)} %bitcast.27, f32[8,128]{1,0:T(8,128)S(1)} %broadcast_1_start_ref.2.start_ref), custom_call_target="tpu_custom_call" | custom-call | flops 4831838208 | bytes 4194304 | tf_op jit(solution)/shard_map/pallas_call | solution.py:90
  115.8 0.0 collective-permute-done
  115.9 2.4 %collective-permute-start.1 = (f32[128,640]{1,0:T(8,128)S(1)}, f32[128,640]{1,0:T(8,128)S(1)}, u32[]{:S(2)}, u32[]{:S(2)}) collective-permute-start(f32[128,640]{1,0:T(8,128)S(1)} %bitcast_add_fusion), channel_id=1, source_target_pairs={{0,64},{32,96},{64,0},{96,32},{1,65},{33,97},{65,1},{97,33},{2,66}... | collective-permute-start | bytes 983048 | tf_op jit(solution)/shard_map/ppermute | solution.py:278
  118.2 9.4 %shard_map.72.start_ref = f32[256,512]{1,0:T(8,128)S(1)} custom-call(f32[32,512,256]{2,1,0:T(8,128)} %slab_ref.7, f32[512,512]{1,0:T(8,128)S(1)} %get-tuple-element.26.factor_ref, f32[4,8,512]{2,1,0:T(8,128)S(1)} %bitcast.28, f32[256,512]{1,0:T(8,128)S(1)} %shard_map.71.start_ref), custom_call_target="tpu_custom_call" | custom-call | flops 9663676416 | bytes 8388608 | tf_op jit(solution)/shard_map/pallas_call | solution.py:90
  127.6 0.0 collective-permute-done.1
  127.7 0.3 collective-permute-start.2
  127.9 6.5 %shard_map.74 = f32[256,512]{1,0:T(8,128)} custom-call(f32[32,512,256]{2,1,0:T(8,128)} %slab_ref.7, f32[512,512]{1,0:T(8,128)S(1)} %get-tuple-element.26.factor_ref, f32[4,8,512]{2,1,0:T(8,128)S(1)} %bitcast.29, f32[256,512]{1,0:T(8,128)S(1)} %shard_map.72.start_ref), custom_call_target="tpu_custom_call" | custom-call | flops 4831838208 | bytes 4194304 | tf_op jit(solution)/shard_map/pallas_call | solution.py:90
  134.4 3.6 %all-to-all-start.5 = ((f32[16,16,512]{2,1,0:T(8,128)}), f32[16,16,512]{2,1,0:T(8,128)S(1)}, u32[]{:S(2)}, u32[]{:S(2)}) async-start(f32[16,16,512]{2,1,0:T(8,128)} %bitcast.15), calls=%async_computation.5 | async-start | bytes 1048576 | tf_op jit(solution)/shard_map/all_to_all | solution.py:263
  138.0 10.7 %shard_map.73 = (f32[512,512]{1,0:T(8,128)S(1)}, f32[1,512]{1,0:T(1,128)}) custom-call(f32[2,128,640]{2,1,0:T(8,128)S(1)} %maximum_select_fusion.strips_ref, f32[128,512]{1,0:T(8,128)S(1)} %bitcast.31), custom_call_target="tpu_custom_call" | custom-call | flops 12000000000 | bytes 1048576 | tf_op jit(solution)/shard_map/pallas_call | solution.py:197
  148.8 0.0 copy-start.5
  148.9 1.0 broadcast_in_dim.11
  149.8 0.1 copy-done.5
  149.9 5.7 %all-to-all-start.6 = ((f32[16,16,512]{2,1,0:T(8,128)}), f32[16,16,512]{2,1,0:T(8,128)S(1)}, u32[]{:S(2)}, u32[]{:S(2)}) async-start(f32[16,16,512]{2,1,0:T(8,128)} %broadcast_in_dim.11), calls=%async_computation.6 | async-start | bytes 1048576 | tf_op jit(solution)/shard_map/all_to_all | solution.py:263
  155.6 0.0 copy-start.6
  155.6 1.2 copy-done.6
  156.8 10.0 %shard_map.75.inverse_ref = f32[512,512]{1,0:T(8,128)S(1)} custom-call(f32[512,512]{1,0:T(8,128)S(1)} %copy-done.6), custom_call_target="tpu_custom_call" | custom-call | flops 12000000000 | bytes 1048576 | tf_op jit(solution)/shard_map/pallas_call | solution.py:217
  166.8 1.1 shard_map.76
  167.9 0.6 reshape.78
  168.5 4.1 %all-to-all-start.7 = ((f32[8,1,512]{2,1,0:T(1,128)}), f32[8,1,512]{2,1,0:T(1,128)S(1)}, u32[]{:S(2)}, u32[]{:S(2)}) async-start(f32[8,1,512]{2,1,0:T(1,128)} %reshape.78), calls=%async_computation.7 | async-start | bytes 32768 | tf_op jit(solution)/shard_map/all_to_all | solution.py:263
  172.6 1.1 broadcast_divide_fusion
  173.8 6.6 %all-to-all-done.7 = f32[8,1,512]{2,1,0:T(1,128)S(1)} async-done(((f32[8,1,512]{2,1,0:T(1,128)}), f32[8,1,512]{2,1,0:T(1,128)S(1)}, u32[]{:S(2)}, u32[]{:S(2)}) %all-to-all-start.7) | async-done | bytes 16416 | tf_op jit(solution)/shard_map/all_to_all | solution.py:263
  180.4 0.0 copy-start.9
  180.4 0.9 broadcast_divide_fusion.1
  (21 shorter events, 0.3 us)
Async XLA Ops:
  0.6 1.0 copy-start.2
  23.8 24.4 %all-to-all-start.2 = ((f32[4,32,512]{2,1,0:T(8,128)}), f32[4,32,512]{2,1,0:T(8,128)S(1)}, u32[]{:S(2)}, u32[]{:S(2)}) async-start(f32[4,32,512]{2,1,0:T(8,128)} %broadcast_in_dim.9), calls=%async_computation.2 | async-start | bytes 524288 | tf_op jit(solution)/shard_map/all_to_all | solution.py:263
  29.1 0.8 copy-start
  29.9 1.0 copy-start.3
  49.1 14.2 %all-to-all-start.1 = ((f32[8,32,640]{2,1,0:T(8,128)}), f32[8,32,640]{2,1,0:T(8,128)S(1)}, u32[]{:S(2)}, u32[]{:S(2)}) async-start(f32[8,32,640]{2,1,0:T(8,128)} %broadcast_in_dim.8), calls=%async_computation.1 | async-start | bytes 1310720 | tf_op jit(solution)/shard_map/all_to_all | solution.py:263
  63.3 21.2 %all-to-all-start.3 = ((f32[32,16,512]{2,1,0:T(8,128)}), f32[32,16,512]{2,1,0:T(8,128)S(1)}, u32[]{:S(2)}, u32[]{:S(2)}) async-start(f32[32,16,512]{2,1,0:T(8,128)} %bitcast.6), calls=%async_computation.3 | async-start | bytes 2097152 | tf_op jit(solution)/shard_map/all_to_all | solution.py:263
  80.3 1.0 copy-start.7
  85.7 21.0 %all-to-all-start.4 = ((f32[32,16,512]{2,1,0:T(8,128)}), f32[32,16,512]{2,1,0:T(8,128)S(1)}, u32[]{:S(2)}, u32[]{:S(2)}) async-start(f32[32,16,512]{2,1,0:T(8,128)} %broadcast_in_dim.10), calls=%async_computation.4 | async-start | bytes 2097152 | tf_op jit(solution)/shard_map/all_to_all | solution.py:263
  92.5 1.2 copy-start.8
  93.7 16.4 %copy-start.1 = (f32[32,512]{1,0:T(8,128)S(1)}, f32[32,512]{1,0:T(8,128)}, u32[]{:S(2)}) copy-start(f32[32,512]{1,0:T(8,128)} %param.5) | copy-start | bytes 196612
  110.0 5.8 %collective-permute-start = (f32[128,640]{1,0:T(8,128)S(1)}, f32[128,640]{1,0:T(8,128)S(1)}, u32[]{:S(2)}, u32[]{:S(2)}) collective-permute-start(f32[128,640]{1,0:T(8,128)S(1)} %dynamic-slice_bitcast_fusion), channel_id=1, source_target_pairs={{0,32},{32,0},{64,96},{96,64},{1,33},{33,1},{65,97},{97,65},{2,34}... | collective-permute-start | bytes 983048 | tf_op jit(solution)/shard_map/ppermute | solution.py:278
  115.9 11.7 %collective-permute-start.1 = (f32[128,640]{1,0:T(8,128)S(1)}, f32[128,640]{1,0:T(8,128)S(1)}, u32[]{:S(2)}, u32[]{:S(2)}) collective-permute-start(f32[128,640]{1,0:T(8,128)S(1)} %bitcast_add_fusion), channel_id=1, source_target_pairs={{0,64},{32,96},{64,0},{96,32},{1,65},{33,97},{65,1},{97,33},{2,66}... | collective-permute-start | bytes 983048 | tf_op jit(solution)/shard_map/ppermute | solution.py:278
  127.7 10.3 %collective-permute-start.2 = (f32[128,640]{1,0:T(8,128)S(1)}, f32[128,640]{1,0:T(8,128)S(1)}, u32[]{:S(2)}, u32[]{:S(2)}) collective-permute-start(f32[128,640]{1,0:T(8,128)S(1)} %add.32), channel_id=1, source_target_pairs={{0,32},{32,0},{64,96},{96,64},{1,33},{33,1},{65,97},{97,65},{2,34}... | collective-permute-start | bytes 983048 | tf_op jit(solution)/shard_map/ppermute | solution.py:278
  134.4 14.4 %all-to-all-start.5 = ((f32[16,16,512]{2,1,0:T(8,128)}), f32[16,16,512]{2,1,0:T(8,128)S(1)}, u32[]{:S(2)}, u32[]{:S(2)}) async-start(f32[16,16,512]{2,1,0:T(8,128)} %bitcast.15), calls=%async_computation.5 | async-start | bytes 1048576 | tf_op jit(solution)/shard_map/all_to_all | solution.py:263
  148.8 1.1 copy-start.5
  149.9 16.9 %all-to-all-start.6 = ((f32[16,16,512]{2,1,0:T(8,128)}), f32[16,16,512]{2,1,0:T(8,128)S(1)}, u32[]{:S(2)}, u32[]{:S(2)}) async-start(f32[16,16,512]{2,1,0:T(8,128)} %broadcast_in_dim.11), calls=%async_computation.6 | async-start | bytes 1048576 | tf_op jit(solution)/shard_map/all_to_all | solution.py:263
  155.6 1.2 copy-start.6
  156.8 10.0 %copy-start.4 = (f32[1,512]{1,0:T(1,128)S(1)}, f32[1,512]{1,0:T(1,128)}, u32[]{:S(2)}) copy-start(f32[1,512]{1,0:T(1,128)} %get-tuple-element.31.scale_ref) | copy-start | bytes 6148
  168.5 11.8 %all-to-all-start.7 = ((f32[8,1,512]{2,1,0:T(1,128)}), f32[8,1,512]{2,1,0:T(1,128)S(1)}, u32[]{:S(2)}, u32[]{:S(2)}) async-start(f32[8,1,512]{2,1,0:T(1,128)} %reshape.78), calls=%async_computation.7 | async-start | bytes 32768 | tf_op jit(solution)/shard_map/all_to_all | solution.py:263
  180.4 0.9 copy-start.9
